TPU v7x, 32 devices: a whole 2x2x4 slice. The times are simulated.
32 devices in a mesh: seq: 4 (over z), batch: 8 (over y, x, core).
Axes of the slice: x: 2, y: 2, z: 4, core: 2. Of those that a mesh axis runs over, the one named last changes fastest.
Arguments:
- tokens: bfloat16 [24, 2048, 512], P('batch', 'seq'), may hold values from -6 to 6
- cotangent: bfloat16 [24, 2048, 512], P('batch', 'seq'), may hold values from -6 to 6
- start_states: float32 [24, 1024], P('batch'), may hold values from -6 to 6
- lengths: int32 [24], P('batch'), may hold values from 1024 to 2048, as said below
- w_in: float32 [512, 2048], P(('seq', 'batch')), may hold values from -0.25 to 0.25
- w_out: float32 [1024, 512], P(('seq', 'batch')), may hold values from -0.1875 to 0.1875
- w_up: float32 [512, 2048], P(('seq', 'batch')), may hold values from -0.25 to 0.25
- w_down: float32 [2048, 512], P(('seq', 'batch')), may hold values from -0.125 to 0.125
- vectors: float32 [4096], P(('seq', 'batch'))
- first_in: float32 [512, 2048], P(('seq', 'batch')), may hold values from -224 to 224
- second_in: float32 [512, 2048], P(('seq', 'batch')), may hold values from 737.28 to 11796.48
- first_out: float32 [1024, 512], P(('seq', 'batch')), may hold values from -640 to 640
- second_out: float32 [1024, 512], P(('seq', 'batch')), may hold values from 6635.52 to 106168.32
- first_up: float32 [512, 2048], P(('seq', 'batch')), may hold values from -320 to 320
- second_up: float32 [512, 2048], P(('seq', 'batch')), may hold values from 1671.168 to 26542.08
- first_down: float32 [2048, 512], P(('seq', 'batch')), may hold values from -640 to 640
- second_down: float32 [2048, 512], P(('seq', 'batch')), may hold values from 6635.52 to 106168.32
- first_vec: float32 [4096], P(('seq', 'batch')), may hold values from -448 to 448
- second_vec: float32 [4096], P(('seq', 'batch')), may hold values from 2949.12 to 47185.92
Outputs:
- block_out: bfloat16 [24, 2048, 512], P('batch', 'seq')
- stretch_states: float32 [24, 4, 1024], P('batch', 'seq')
- grad_tokens: float32 [24, 2048, 512], P('batch', 'seq')
- new_in: float32 [512, 2048], P(('seq', 'batch'))
- copy_in: bfloat16 [512, 2048], P(('seq', 'batch'))
- moment_in: float32 [512, 2048], P(('seq', 'batch'))
- square_in: float32 [512, 2048], P(('seq', 'batch'))
- new_out: float32 [1024, 512], P(('seq', 'batch'))
- copy_out: bfloat16 [1024, 512], P(('seq', 'batch'))
- moment_out: float32 [1024, 512], P(('seq', 'batch'))
- square_out: float32 [1024, 512], P(('seq', 'batch'))
- new_up: float32 [512, 2048], P(('seq', 'batch'))
- copy_up: bfloat16 [512, 2048], P(('seq', 'batch'))
- moment_up: float32 [512, 2048], P(('seq', 'batch'))
- square_up: float32 [512, 2048], P(('seq', 'batch'))
- new_down: float32 [2048, 512], P(('seq', 'batch'))
- copy_down: bfloat16 [2048, 512], P(('seq', 'batch'))
- moment_down: float32 [2048, 512], P(('seq', 'batch'))
- square_down: float32 [2048, 512], P(('seq', 'batch'))
- new_vec: float32 [4096], P(('seq', 'batch'))
- moment_vec: float32 [4096], P(('seq', 'batch'))
- square_vec: float32 [4096], P(('seq', 'batch'))
Inputs may be any that keep to these rules, and one draw needn't show every extreme that they name: `lengths`: in every group of 3 consecutive sequences one has length exactly 2048.
All inputs are finite; a program needn't handle non-finite values.
Results may differ from a plain program's by a relative error of at most 0.012.
The roundings to bfloat16 on the way count: a program that leaves them out, or rounds other values in their place, can miss the bound.
Values may be sent and summed in bfloat16 or wider, within the bound.
A program may use at most 192 MiB of HBM per device.

v0:
```python
import jax
import jax.numpy as jnp
from jax import lax
from jax.sharding import PartitionSpec as P

D = 512
H = 1024
F = 2048
STEP = 5


EPS = 1e-06
ADAM_EPS = 1e-08
BETA_ONE = 0.5
BETA_TWO = 0.5
DECAY = 0.1
VEC_RATE = 1.5


def entering_2(value, axis, combine, identity, reverse):
    size, mine = (lax.axis_size(axis), lax.axis_index(axis))
    everything = jax.tree.map(lambda part: lax.all_gather(part, axis), value)
    start = jax.tree.map(
        lambda part, zero: jnp.broadcast_to(jnp.asarray(zero, part.dtype), part.shape),
        value,
        identity,
    )

    def step(k, before):
        at = size - 1 - k if reverse else k
        reached = at > mine if reverse else at < mine
        new = combine(before, jax.tree.map(lambda part: part[at], everything))
        return jax.tree.map(lambda a, b: jnp.where(reached, a, b), new, before)

    return lax.fori_loop(0, size, step, start)


def shifted_2(value, axis, by):
    size = lax.axis_size(axis)
    pairs = [(i, i + by) for i in range(size) if 0 <= i + by < size]
    return lax.ppermute(value, axis, pairs)


def combine_affine(earlier, later):
    return (earlier[0] * later[0], later[0] * earlier[1] + later[1])


def carry_forward(keep_total, drive_total):
    return entering_2(
        (keep_total, drive_total),
        "seq",
        combine_affine,
        (jnp.ones_like(keep_total), jnp.zeros_like(drive_total)),
        False,
    )


def carry_backward(keep_total, drive_total):
    return entering_2(
        (keep_total, drive_total),
        "seq",
        combine_affine,
        (jnp.ones_like(keep_total), jnp.zeros_like(drive_total)),
        True,
    )


def adam_step(weight, grad, first, second, rate, decay):
    moment = BETA_ONE * first + (1.0 - BETA_ONE) * grad
    square = BETA_TWO * second + (1.0 - BETA_TWO) * grad * grad
    corr_one = 1.0 - BETA_ONE**STEP
    corr_two = 1.0 - BETA_TWO**STEP
    direction = moment / corr_one / (jnp.sqrt(square / corr_two) + ADAM_EPS)
    fresh = weight - rate * (direction + decay * weight)
    return (fresh, moment, square)


def shards(
    tokens,
    cotangent,
    start_states,
    lengths,
    w_in,
    w_out,
    w_up,
    w_down,
    vectors,
    first_in,
    second_in,
    first_out,
    second_out,
    first_up,
    second_up,
    first_down,
    second_down,
    first_vec,
    second_vec,
):
    f32 = jnp.float32
    bf16 = jnp.bfloat16
    full_in, full_out, full_up, full_down, full_vec = (
        lax.all_gather(w_in.astype(bf16), ("seq", "batch"), axis=0, tiled=True),
        lax.all_gather(w_out.astype(bf16), ("seq", "batch"), axis=0, tiled=True),
        lax.all_gather(w_up.astype(bf16), ("seq", "batch"), axis=0, tiled=True),
        lax.all_gather(w_down.astype(bf16), ("seq", "batch"), axis=0, tiled=True),
        lax.all_gather(vectors.astype(bf16), ("seq", "batch"), axis=0, tiled=True),
    )
    vec_full = full_vec.astype(f32)
    g_one = vec_full[:D]
    g_two = vec_full[D : 2 * D]
    taps = vec_full[2 * D : 6 * D].reshape(4, D)
    bias = vec_full[6 * D :]
    span_len = tokens.shape[1]
    offset = lax.axis_index("seq") * span_len
    valid = ((offset + jnp.arange(span_len))[None, :] < lengths[:, None]).astype(f32)[..., None]
    inputs = tokens.astype(f32)
    scale_one = lax.rsqrt(jnp.mean(inputs * inputs, axis=-1, keepdims=True) + EPS)
    unit_one = inputs * scale_one
    normed = (unit_one * g_one).astype(bf16)
    rim_in = shifted_2(normed[:, span_len - 3 :, :], "seq", 1)
    extended = jnp.concatenate([rim_in, normed], axis=1).astype(f32)
    mixed = sum((taps[tap_idx] * extended[:, tap_idx : tap_idx + span_len] for tap_idx in range(4)))
    mixed_low = mixed.astype(bf16)
    projected = jnp.einsum("scd,dk->sck", mixed_low, full_in, preferred_element_type=f32)
    cand = projected[..., H:]
    gate_sig = jax.nn.sigmoid(projected[..., :H] + bias)
    update = gate_sig * valid
    retain = 1.0 - update
    driven = update * cand
    run_keep, run_drive = lax.associative_scan(combine_affine, (retain, driven), axis=1)
    enter_keep, enter_drive = carry_forward(run_keep[:, -1], run_drive[:, -1])
    entering = enter_keep * start_states + enter_drive
    states = run_keep * entering[:, None] + run_drive
    stretch_end = states[:, span_len - 1 :]
    state_low = states.astype(bf16)
    mixer = jnp.einsum("sch,hd->scd", state_low, full_out, preferred_element_type=f32)
    middle = inputs + valid * mixer
    scale_two = lax.rsqrt(jnp.mean(middle * middle, axis=-1, keepdims=True) + EPS)
    unit_two = middle * scale_two
    normed_two = (unit_two * g_two).astype(bf16)
    up_pre = jnp.einsum("scd,df->scf", normed_two, full_up, preferred_element_type=f32)
    gelu_out, gelu_pull = jax.vjp(jax.nn.gelu, up_pre)
    gelu_low = gelu_out.astype(bf16)
    branch = jnp.einsum("scf,fd->scd", gelu_low, full_down, preferred_element_type=f32)
    block_out = (middle + valid * branch).astype(bf16)
    grad_y = cotangent.astype(f32)
    d_branch = (grad_y * valid).astype(bf16)
    grad_down = jnp.einsum("scf,scd->fd", gelu_low, d_branch, preferred_element_type=f32)
    d_gelu = jnp.einsum("scd,fd->scf", d_branch, full_down, preferred_element_type=f32)
    d_up = gelu_pull(d_gelu)[0].astype(bf16)
    grad_up = jnp.einsum("scd,scf->df", normed_two, d_up, preferred_element_type=f32)
    d_normed_two = jnp.einsum("scf,df->scd", d_up, full_up, preferred_element_type=f32)
    grad_g_two = jnp.sum(d_normed_two * unit_two, axis=(0, 1))
    e_two = d_normed_two * g_two
    d_middle = grad_y + scale_two * (
        e_two - unit_two * jnp.mean(e_two * unit_two, axis=-1, keepdims=True)
    )
    d_mixer = (d_middle * valid).astype(bf16)
    grad_out = jnp.einsum("sch,scd->hd", state_low, d_mixer, preferred_element_type=f32)
    d_states = jnp.einsum("scd,hd->sch", d_mixer, full_out, preferred_element_type=f32)
    shifted = jnp.concatenate([retain[:, 1:], jnp.ones_like(retain[:, :1])], axis=1)
    back_keep, back_drive = lax.associative_scan(
        combine_affine, (shifted, d_states), axis=1, reverse=True
    )
    send_keep = retain[:, 0] * back_keep[:, 0]
    send_drive = retain[:, 0] * back_drive[:, 0]
    unused_keep, incoming = carry_backward(send_keep, send_drive)
    adjoint = back_keep * incoming[:, None] + back_drive
    prev_state = jnp.concatenate([entering[:, None], states[:, :-1]], axis=1)
    d_update = adjoint * (cand - prev_state)
    d_gate = d_update * valid * gate_sig * (1.0 - gate_sig)
    grad_bias = jnp.sum(d_gate, axis=(0, 1))
    gate_low = d_gate.astype(bf16)
    cand_low = (adjoint * update).astype(bf16)
    grad_in = jnp.concatenate(
        [
            jnp.einsum("scd,sck->dk", mixed_low, gate_low, preferred_element_type=f32),
            jnp.einsum("scd,sck->dk", mixed_low, cand_low, preferred_element_type=f32),
        ],
        axis=1,
    )
    d_mixed = jnp.einsum(
        "sck,dk->scd", gate_low, full_in[:, :H], preferred_element_type=f32
    ) + jnp.einsum("sck,dk->scd", cand_low, full_in[:, H:], preferred_element_type=f32)
    grad_taps = jnp.stack(
        [
            jnp.sum(d_mixed * extended[:, tap_idx : tap_idx + span_len], axis=(0, 1))
            for tap_idx in range(4)
        ]
    )
    rim_terms = jnp.stack(
        [
            sum((taps[tap_idx] * d_mixed[:, lead - tap_idx] for tap_idx in range(lead + 1)))
            for lead in range(3)
        ],
        axis=1,
    )
    mixed_tail = jnp.concatenate([d_mixed, jnp.zeros_like(d_mixed[:, :3])], axis=1)
    d_normed = sum(
        (
            taps[tap_idx] * mixed_tail[:, 3 - tap_idx : 3 - tap_idx + span_len]
            for tap_idx in range(4)
        )
    )
    rim_back = shifted_2(rim_terms, "seq", -1)
    d_normed = d_normed.at[:, span_len - 3 :].add(rim_back)
    grad_g_one = jnp.sum(d_normed * unit_one, axis=(0, 1))
    e_one = d_normed * g_one
    grad_tokens = d_middle + scale_one * (
        e_one - unit_one * jnp.mean(e_one * unit_one, axis=-1, keepdims=True)
    )
    grad_vec = jnp.concatenate([grad_g_one, grad_g_two, grad_taps.reshape(-1), grad_bias])
    sum_in, sum_out, sum_up, sum_down, sum_vec = (
        lax.psum_scatter(grad_in, ("seq", "batch"), scatter_dimension=0, tiled=True),
        lax.psum_scatter(grad_out, ("seq", "batch"), scatter_dimension=0, tiled=True),
        lax.psum_scatter(grad_up, ("seq", "batch"), scatter_dimension=0, tiled=True),
        lax.psum_scatter(grad_down, ("seq", "batch"), scatter_dimension=0, tiled=True),
        lax.psum_scatter(grad_vec, ("seq", "batch"), scatter_dimension=0, tiled=True),
    )
    new_in, moment_in, square_in = adam_step(w_in, sum_in, first_in, second_in, D ** (-0.5), DECAY)
    new_out, moment_out, square_out = adam_step(
        w_out, sum_out, first_out, second_out, H ** (-0.5), DECAY
    )
    new_up, moment_up, square_up = adam_step(w_up, sum_up, first_up, second_up, D ** (-0.5), DECAY)
    new_down, moment_down, square_down = adam_step(
        w_down, sum_down, first_down, second_down, F ** (-0.5), DECAY
    )
    new_vec, moment_vec, square_vec = adam_step(
        vectors, sum_vec, first_vec, second_vec, VEC_RATE, 0.0
    )
    return (
        block_out,
        stretch_end,
        grad_tokens,
        new_in,
        new_in.astype(bf16),
        moment_in,
        square_in,
        new_out,
        new_out.astype(bf16),
        moment_out,
        square_out,
        new_up,
        new_up.astype(bf16),
        moment_up,
        square_up,
        new_down,
        new_down.astype(bf16),
        moment_down,
        square_down,
        new_vec,
        moment_vec,
        square_vec,
    )


def solution(mesh):
    placed = (
        P("batch", "seq", None),
        P("batch", "seq", None),
        P("batch", None),
        P("batch"),
        P(("seq", "batch"), None),
        P(("seq", "batch"), None),
        P(("seq", "batch"), None),
        P(("seq", "batch"), None),
        P(("seq", "batch")),
        P(("seq", "batch"), None),
        P(("seq", "batch"), None),
        P(("seq", "batch"), None),
        P(("seq", "batch"), None),
        P(("seq", "batch"), None),
        P(("seq", "batch"), None),
        P(("seq", "batch"), None),
        P(("seq", "batch"), None),
        P(("seq", "batch")),
        P(("seq", "batch")),
    )
    return jax.shard_map(
        shards,
        mesh=mesh,
        in_specs=placed,
        out_specs=(
            P("batch", "seq", None),
            P("batch", "seq", None),
            P("batch", "seq", None),
            P(("seq", "batch"), None),
            P(("seq", "batch"), None),
            P(("seq", "batch"), None),
            P(("seq", "batch"), None),
            P(("seq", "batch"), None),
            P(("seq", "batch"), None),
            P(("seq", "batch"), None),
            P(("seq", "batch"), None),
            P(("seq", "batch"), None),
            P(("seq", "batch"), None),
            P(("seq", "batch"), None),
            P(("seq", "batch"), None),
            P(("seq", "batch"), None),
            P(("seq", "batch"), None),
            P(("seq", "batch"), None),
            P(("seq", "batch"), None),
            P(("seq", "batch")),
            P(("seq", "batch")),
            P(("seq", "batch")),
        ),
        check_vma=False,
    )
```

profile of v0, /device:TPU:0, one launch (start us, length us, event | category | flops | bytes accessed | tf_op | source)
XLA Modules:
  0.0 1372.0 jit_solution(9687627992327079333)
XLA Ops:
  11.1 43.0 %all-gather.4 = bf16[32,1,128]{2,1,0:T(2,128)(2,1)S(1)} all-gather(bf16[1,1,128]{2,1,0:T(2,128)(2,1)S(1)} %convert_bitcast_fusion), channel_id=1, replica_groups=mesh['seq'=4,'batch'=8] {'seq','batch'}, dimensions={0}, use_global_device_ids=true | all-gather | bytes 8448 | tf_op jit(solution)/shard_map/all_gather | solution.py:106
  75.8 6.1 multiply_subtract_fusion
  84.1 14.4 %slice.776 = f32[3,255,1024]{2,1,0:T(8,128)} slice(f32[3,512,1024]{2,1,0:T(8,128)} %get-tuple-element.439), slice={[0:3:1], [2:512:2], [0:1024:1]} | slice | bytes 6266880 | tf_op jit(solution)/shard_map/slice | solution.py:130
  98.5 14.2 %slice.737 = f32[3,256,1024]{2,1,0:T(8,128)} slice(f32[3,512,1024]{2,1,0:T(8,128)} %get-tuple-element.439), slice={[0:3:1], [1:512:2], [0:1024:1]} | slice | bytes 6291456 | tf_op jit(solution)/shard_map/slice | solution.py:130
  112.7 14.2 %slice.736 = f32[3,256,1024]{2,1,0:T(8,128)} slice(f32[3,512,1024]{2,1,0:T(8,128)} %get-tuple-element.439), slice={[0:3:1], [0:511:2], [0:1024:1]} | slice | bytes 6291456 | tf_op jit(solution)/shard_map/slice | solution.py:130
  126.9 14.4 %slice.732 = f32[3,255,1024]{2,1,0:T(8,128)} slice(f32[3,512,1024]{2,1,0:T(8,128)} %get-tuple-element.438), slice={[0:3:1], [2:512:2], [0:1024:1]} | slice | bytes 6266880 | tf_op jit(solution)/shard_map/slice | solution.py:130
  141.3 14.1 %slice.693 = f32[3,256,1024]{2,1,0:T(8,128)} slice(f32[3,512,1024]{2,1,0:T(8,128)} %get-tuple-element.438), slice={[0:3:1], [1:512:2], [0:1024:1]} | slice | bytes 6291456 | tf_op jit(solution)/shard_map/slice | solution.py:130
  155.4 14.2 %slice.692 = f32[3,256,1024]{2,1,0:T(8,128)} slice(f32[3,512,1024]{2,1,0:T(8,128)} %get-tuple-element.438), slice={[0:3:1], [0:511:2], [0:1024:1]} | slice | bytes 6291456 | tf_op jit(solution)/shard_map/slice | solution.py:130
  169.7 6.3 fusion.92
  178.3 7.8 slice.730
  186.1 7.6 slice.696
  193.7 7.6 slice.695
  276.4 7.7 pad.239
  284.1 7.7 pad.240
  291.8 7.7 pad.258
  299.5 11.1 add_multiply_fusion.3
  321.3 15.2 %pad.259 = f32[3,512,1024]{2,1,0:T(8,128)} pad(f32[3,256,1024]{2,1,0:T(8,128)} %pad_maximum_fusion.2, f32[]{:T(128)} %constant.148.clone.1), padding=0_0_0x0_1_1x0_0_0 | pad | bytes 9437188 | tf_op jit(solution)/shard_map/pad | solution.py:130
  338.6 14.6 %pad.241 = f32[3,512,1024]{2,1,0:T(8,128)} pad(f32[3,256,1024]{2,1,0:T(8,128)} %pad_maximum_fusion.1, f32[]{:T(128)} %constant.148.clone.1), padding=0_0_0x0_1_1x0_0_0 | pad | bytes 9437188 | tf_op jit(solution)/shard_map/pad | solution.py:130
  353.2 15.3 %pad.242 = f32[3,512,1024]{2,1,0:T(8,128)} pad(f32[3,256,1024]{2,1,0:T(8,128)} %add.630, f32[]{:T(128)} %constant.148.clone.1), padding=0_0_0x1_0_1x0_0_0 | pad | bytes 9437188 | tf_op jit(solution)/shard_map/pad | solution.py:130
  369.5 13.1 all-gather
  382.8 9.6 pad.260
  393.3 13.1 all-gather.1
  406.9 12.8 multiply_add_fusion.1
  419.8 6.8 multiply_reduce_fusion.6
  426.6 6.1 fusion.37
  437.4 7.7 convolution_bitcast_fusion
  445.2 140.0 %reduce-scatter.11.cloned.1.call-done = f32[64,512]{1,0:T(8,128)} async-done(((f32[2048,512]{1,0:T(8,128)}), f32[64,512]{1,0:T(8,128)}) %reduce-scatter.11.cloned.1.call-update) | async-done | bytes 131088 | tf_op jit(solution)/shard_map/reduce_scatter | solution.py:217
  594.6 14.2 %slice.823 = f32[3,255,1024]{2,1,0:T(8,128)} slice(f32[3,512,1024]{2,1,0:T(8,128)} %concatenate.133), slice={[0:3:1], [1:510:2], [0:1024:1]} | slice | bytes 6266880 | tf_op jit(solution)/shard_map/slice | solution.py:162
  608.8 12.1 slice.783
  620.9 14.3 %slice.781 = f32[3,256,1024]{2,1,0:T(8,128)} slice(f32[3,512,1024]{2,1,0:T(8,128)} %concatenate.133), slice={[0:3:1], [1:512:2], [0:1024:1]} | slice | bytes 6291456 | tf_op jit(solution)/shard_map/slice | solution.py:162
  635.1 25.3 %slice.824 = f32[3,255,1024]{2,1,0:T(8,128)} reverse(f32[3,255,1024]{2,1,0:T(8,128)} %slice.823), dimensions={1} | reverse | bytes 6266880 | tf_op jit(solution)/shard_map/slice | solution.py:162
  660.4 24.7 %slice.782 = f32[3,256,1024]{2,1,0:T(8,128)} reverse(f32[3,256,1024]{2,1,0:T(8,128)} %slice.781), dimensions={1} | reverse | bytes 6291456 | tf_op jit(solution)/shard_map/slice | solution.py:162
  685.1 15.6 %slice.784 = f32[3,256,1024]{2,1,0:T(8,128)} reverse(f32[3,256,1024]{2,1,0:T(8,128)S(1)} %slice.783), dimensions={1} | reverse | bytes 6291456 | tf_op jit(solution)/shard_map/slice | solution.py:162
  700.8 13.6 fusion.8
  720.5 7.1 convolution_bitcast_fusion.2
  733.9 14.2 %slice.869 = f32[3,255,1024]{2,1,0:T(8,128)} slice(f32[3,512,1024]{2,1,0:T(8,128)} %copy-done.3), slice={[0:3:1], [1:510:2], [0:1024:1]} | slice | bytes 6266880 | tf_op jit(solution)/shard_map/slice | solution.py:162
  748.1 12.1 slice.829
  760.2 14.2 %slice.827 = f32[3,256,1024]{2,1,0:T(8,128)} slice(f32[3,512,1024]{2,1,0:T(8,128)} %copy-done.3), slice={[0:3:1], [1:512:2], [0:1024:1]} | slice | bytes 6291456 | tf_op jit(solution)/shard_map/slice | solution.py:162
  774.3 24.7 %slice.828 = f32[3,256,1024]{2,1,0:T(8,128)} reverse(f32[3,256,1024]{2,1,0:T(8,128)} %slice.827), dimensions={1} | reverse | bytes 6291456 | tf_op jit(solution)/shard_map/slice | solution.py:162
  799.1 15.6 %slice.830 = f32[3,256,1024]{2,1,0:T(8,128)} reverse(f32[3,256,1024]{2,1,0:T(8,128)S(1)} %slice.829), dimensions={1} | reverse | bytes 6291456 | tf_op jit(solution)/shard_map/slice | solution.py:162
  814.7 6.1 fusion.91
  823.1 7.8 slice.821
  830.9 7.6 slice.787
  838.5 7.6 slice.786
  903.2 16.6 %slice.870 = f32[3,255,1024]{2,1,0:T(8,128)} reverse(f32[3,255,1024]{2,1,0:T(8,128)S(1)} %copy-done.19), dimensions={1} | reverse | bytes 6266880 | tf_op jit(solution)/shard_map/slice | solution.py:162
  922.9 9.4 convolution_bitcast_fusion.1
  969.3 7.6 pad.275
  977.0 7.7 pad.276
  984.7 7.8 pad.294
  999.2 9.6 add_multiply_fusion.1
  1013.9 14.6 %pad.295 = f32[3,512,1024]{2,1,0:T(8,128)} pad(f32[3,256,1024]{2,1,0:T(8,128)} %pad_maximum_fusion.3, f32[]{:T(128)} %constant.148.clone.1), padding=0_0_0x0_1_1x0_0_0 | pad | bytes 9437188 | tf_op jit(solution)/shard_map/pad | solution.py:162
  1028.5 9.5 pad.277
  1038.0 15.2 %pad.278 = f32[3,512,1024]{2,1,0:T(8,128)} pad(f32[3,256,1024]{2,1,0:T(8,128)} %add.673, f32[]{:T(128)} %constant.148.clone.1), padding=0_0_0x1_0_1x0_0_0 | pad | bytes 9437188 | tf_op jit(solution)/shard_map/pad | solution.py:162
  1053.2 9.9 pad.296
  1063.1 9.5 add.700
  1072.6 48.6 %rev.9 = f32[3,512,1024]{2,1,0:T(8,128)} reverse(f32[3,512,1024]{2,1,0:T(8,128)} %add.700), dimensions={1} | reverse | bytes 12582912 | tf_op jit(solution)/shard_map/rev | solution.py:162
  1121.2 9.5 add.674
  1130.7 48.5 %rev.8 = f32[3,512,1024]{2,1,0:T(8,128)} reverse(f32[3,512,1024]{2,1,0:T(8,128)} %add.674), dimensions={1} | reverse | bytes 12582912 | tf_op jit(solution)/shard_map/rev | solution.py:162
  1180.3 13.1 all-gather.3
  1193.5 13.1 all-gather.2
  1207.0 11.9 fusion.81
  1237.8 8.0 add_convert_fusion
  1248.5 40.7 %all-reduce.75 = f32[4096]{0:T(1024)S(1)} all-reduce(f32[4096]{0:T(1024)S(1)} %pad_maximum_fusion.33), channel_id=10, replica_groups=mesh['seq'=4,'batch'=8] {'seq','batch'}, use_global_device_ids=true, to_apply=%region_19.20.clone | all-reduce | flops 4096 | bytes 32768
  1297.2 65.6 %reduce-scatter.5.cloned.1.call-done = f32[16,2048]{1,0:T(8,128)} async-done(((f32[512,2048]{1,0:T(8,128)}), f32[16,2048]{1,0:T(8,128)}) %reduce-scatter.5.cloned.1.call-update) | async-done | bytes 131088 | tf_op jit(solution)/shard_map/reduce_scatter | solution.py:214
  (553 shorter events, 289.6 us)
Async XLA Ops:
  7.2 53.0 %copy-start.53 = (f32[16,2048]{1,0:T(8,128)S(1)}, f32[16,2048]{1,0:T(8,128)}, u32[]{:S(2)}) copy-start(f32[16,2048]{1,0:T(8,128)} %param.31) | copy-start | bytes 393220
  7.2 53.7 %copy-start.102 = (s32[3]{0:T(128)S(1)}, s32[3]{0:T(128)}, u32[]{:S(2)}) copy-start(s32[3]{0:T(128)} %param.28) | copy-start | bytes 40
  7.2 63.4 %all-gather.10.cloned.1.call-start = ((), (), s32[]{:S(2)}) async-start(), calls=%async_computation.4 | async-start | bytes 2162688 | tf_op jit(solution)/shard_map/all_gather | solution.py:102
  8.8 410.9 %all-gather.12.cloned.1.call-start = ((), (), s32[]{:S(2)}) async-start(), calls=%async_computation.5 | async-start | bytes 1081344 | tf_op jit(solution)/shard_map/all_gather | solution.py:103
  10.4 416.2 %all-gather.14.cloned.1.call-start = ((), (), s32[]{:S(2)}) async-start(), calls=%async_computation.6 | async-start | bytes 2162688 | tf_op jit(solution)/shard_map/all_gather | solution.py:104
  56.4 5.7 copy-start.89
  56.4 5.7 copy-start.91
  56.4 5.7 copy-start.93
  56.4 5.7 copy-start.95
  58.9 2.7 collective-permute-start
  60.9 524.3 %reduce-scatter.11.cloned.1.call-start = ((), (), s32[]{:S(2)}) async-start(), calls=%async_computation.11 | async-start | bytes 4325376 | tf_op jit(solution)/shard_map/reduce_scatter | solution.py:217
  61.0 14.7 %copy-start.59 = (f32[3,512]{1,0:T(4,128)}, f32[3,512]{1,0:T(4,128)S(1)}, u32[]{:S(2)}) copy-start(f32[3,512]{1,0:T(4,128)S(1)} %compare_convert_fusion) | copy-start | bytes 18436
  61.0 14.7 %copy-start.84 = (f32[8,1,128]{2,1,0:T(1,128)}, f32[8,1,128]{2,1,0:T(1,128)S(1)}, u32[]{:S(2)}) copy-start(f32[8,1,128]{2,1,0:T(1,128)S(1)} %slice.900) | copy-start | bytes 12292
  65.1 10.6 copy-start.17
  75.7 8.4 copy-start.2
  225.4 7.2 copy-start.40
  225.4 7.2 copy-start.41
  269.1 4.3 copy-start.71
  299.5 12.9 copy-start.8
  321.3 15.2 %copy-start.21 = (f32[3,255,1024]{2,1,0:T(8,128)S(1)}, f32[3,255,1024]{2,1,0:T(8,128)}, u32[]{:S(2)}) copy-start(f32[3,255,1024]{2,1,0:T(8,128)} %get-tuple-element.450) | copy-start | bytes 9400324
  353.2 29.5 %copy-start.27 = (f32[3,256,1024]{2,1,0:T(8,128)S(1)}, f32[3,256,1024]{2,1,0:T(8,128)}, u32[]{:S(2)}) copy-start(f32[3,256,1024]{2,1,0:T(8,128)} %add.655) | copy-start | bytes 9437188
  382.7 23.8 %copy-start.52 = (f32[3,1024]{1,0:T(4,128)S(1)}, f32[3,1024]{1,0:T(4,128)}, u32[]{:S(2)}) copy-start(f32[3,1024]{1,0:T(4,128)} %custom-call) | copy-start | bytes 36868
  382.7 24.1 %copy-start.97 = (f32[3,1024]{1,0:T(4,128)S(1)}, f32[3,1024]{1,0:T(4,128)}, u32[]{:S(2)}) copy-start(f32[3,1024]{1,0:T(4,128)} %param.27) | copy-start | bytes 36868
  406.9 12.8 copy-start.10
  406.9 12.8 copy-start.60
  419.7 6.8 copy-start.67
  426.6 10.8 copy-start.45
  432.7 4.6 copy-start.106
  445.1 140.1 %copy-start.63 = (f32[64,512]{1,0:T(8,128)S(1)}, f32[64,512]{1,0:T(8,128)}, u32[]{:S(2)}) copy-start(f32[64,512]{1,0:T(8,128)} %param.32) | copy-start | bytes 393220
  445.1 140.1 %copy-start.64 = (f32[64,512]{1,0:T(8,128)S(1)}, f32[64,512]{1,0:T(8,128)}, u32[]{:S(2)}) copy-start(f32[64,512]{1,0:T(8,128)} %param.40) | copy-start | bytes 393220
  445.1 140.1 %copy-start.65 = (f32[64,512]{1,0:T(8,128)S(1)}, f32[64,512]{1,0:T(8,128)}, u32[]{:S(2)}) copy-start(f32[64,512]{1,0:T(8,128)} %param.41) | copy-start | bytes 393220
  445.1 255.7 %all-gather.16.cloned.1.call-start = ((), (), s32[]{:S(2)}) async-start(), calls=%async_computation.7 | async-start | bytes 2162688 | tf_op jit(solution)/shard_map/all_gather | solution.py:105
  586.9 706.8 %reduce-scatter.7.cloned.1.call-start = ((), (), s32[]{:S(2)}) async-start(), calls=%async_computation.9 | async-start | bytes 2162688 | tf_op jit(solution)/shard_map/reduce_scatter | solution.py:215
  700.8 13.6 copy-start.24
  700.8 13.7 copy-start.105
  714.4 4.7 copy-start.29
  714.5 4.7 copy-start.25
  714.5 4.7 copy-start.46
  720.5 7.1 copy-start.9
  859.6 435.8 %reduce-scatter.9.cloned.1.call-start = ((), (), s32[]{:S(2)}) async-start(), calls=%async_computation.10 | async-start | bytes 4325376 | tf_op jit(solution)/shard_map/reduce_scatter | solution.py:216
  870.4 7.2 copy-start.42
  870.4 7.2 copy-start.43
  885.8 17.5 %copy-start.19 = (f32[3,255,1024]{2,1,0:T(8,128)S(1)}, f32[3,255,1024]{2,1,0:T(8,128)}, u32[]{:S(2)}) copy-start(f32[3,255,1024]{2,1,0:T(8,128)} %slice.869) | copy-start | bytes 9400324
  903.2 17.9 %copy-start.58 = (f32[3,3,1024]{2,1,0:T(4,128)S(1)}, f32[3,3,1024]{2,1,0:T(4,128)}, u32[]{:S(2)}) copy-start(f32[3,3,1024]{2,1,0:T(4,128)} %slice.811) | copy-start | bytes 110596
  932.3 430.5 %reduce-scatter.5.cloned.1.call-start = ((), (), s32[]{:S(2)}) async-start(), calls=%async_computation.8 | async-start | bytes 4325376 | tf_op jit(solution)/shard_map/reduce_scatter | solution.py:214
  962.1 4.3 copy-start.69
  992.4 4.5 copy-start.6
  992.4 4.5 copy-start.7
  1038.0 15.2 %copy-start.28 = (f32[3,256,1024]{2,1,0:T(8,128)S(1)}, f32[3,256,1024]{2,1,0:T(8,128)}, u32[]{:S(2)}) copy-start(f32[3,256,1024]{2,1,0:T(8,128)} %add.698) | copy-start | bytes 9437188
  1130.7 76.0 %copy-start.51 = (f32[3,1024]{1,0:T(4,128)S(1)}, f32[3,1024]{1,0:T(4,128)}, u32[]{:S(2)}) copy-start(f32[3,1024]{1,0:T(4,128)} %custom-call.2) | copy-start | bytes 36868
  1130.7 76.3 %copy-start.68 = (f32[3,1,1024]{2,1,0:T(1,128)S(1)}, f32[3,1,1024]{2,1,0:T(1,128)}, u32[]{:S(2)}) copy-start(f32[3,1,1024]{2,1,0:T(1,128)} %broadcast_in_dim.5) | copy-start | bytes 36868
  1130.7 76.3 %copy-start.85 = (f32[8,1,128]{2,1,0:T(1,128)S(1)}, f32[8,1,128]{2,1,0:T(1,128)}, u32[]{:S(2)}) copy-start(f32[8,1,128]{2,1,0:T(1,128)} %copy-done.84) | copy-start | bytes 12292
  1207.0 12.0 copy-start.18
  1233.0 4.7 copy-start.26
  1233.0 4.7 copy-start.104
  1233.1 12.8 collective-permute-start.1
  1237.8 8.3 copy-start.62
  1237.8 8.3 copy-start.87
  1245.8 43.3 %copy-start.99 = (f32[128]{0:T(128)S(1)}, f32[128]{0:T(128)}, u32[]{:S(2)}) copy-start(f32[128]{0:T(128)} %param.33) | copy-start | bytes 1540
  1245.8 43.3 %copy-start.100 = (f32[128]{0:T(128)S(1)}, f32[128]{0:T(128)}, u32[]{:S(2)}) copy-start(f32[128]{0:T(128)} %param.42) | copy-start | bytes 1540
  1245.8 43.3 %copy-start.101 = (f32[128]{0:T(128)S(1)}, f32[128]{0:T(128)}, u32[]{:S(2)}) copy-start(f32[128]{0:T(128)} %param.43) | copy-start | bytes 1540
  1245.8 43.9 %copy-start.88 = (f32[4,1,128]{2,1,0:T(1,128)S(1)}, f32[4,1,128]{2,1,0:T(1,128)}, u32[]{:S(2)}) copy-start(f32[4,1,128]{2,1,0:T(1,128)} %copy-done.86) | copy-start | bytes 6148
  1289.8 5.6 copy-start.54
  1289.8 73.1 %copy-start.55 = (f32[16,2048]{1,0:T(8,128)S(1)}, f32[16,2048]{1,0:T(8,128)}, u32[]{:S(2)}) copy-start(f32[16,2048]{1,0:T(8,128)} %param.29) | copy-start | bytes 393220
  (53 other events, 109.1 us)
Sparse Core Ops, SparseCore 0:
  11.5 59.0 all-gather.9
  74.0 52.4 all-gather.11
  130.0 55.3 all-gather.13
  445.2 139.8 reduce-scatter.10
  588.4 52.2 all-gather.15
  859.7 132.1 reduce-scatter.6
  994.3 136.8 reduce-scatter.8
  1225.4 137.3 reduce-scatter.4
where the time goes:
time: 1400 us; the launch traced here: 1370 us
  local copies, waits for them, and re-layouts  736 us (53%)
  waiting for transfers between devices  212 us (15%)
  other arithmetic  186 us (13%)
  blocking collectives  136 us (10%)
  matrix products  81.3 us (6%)
  between operations  16.8 us (1%)
    slice x65, local copies, waits for them, and re-layouts, shards(): lax.associative_scan(combine_affine, (shifted, d_states), axis=1, reverse...  276 us
    slice x60, local copies, waits for them, and re-layouts, shards(): lax.associative_scan(combine_affine, (retain, driven), axis=1)  143 us
    reduce_scatter x1, waiting for transfers between devices, shards(): lax.psum_scatter(grad_down, ('seq', 'batch'), scatter_dimension=0, tiled=...  140 us
    rev x2, local copies, waits for them, and re-layouts, shards(): lax.associative_scan(combine_affine, (shifted, d_states), axis=1, reverse...  97 us
    pad x32, local copies, waits for them, and re-layouts, shards(): lax.associative_scan(combine_affine, (retain, driven), axis=1)  95 us
    pad x32, local copies, waits for them, and re-layouts, shards(): lax.associative_scan(combine_affine, (shifted, d_states), axis=1, reverse...  89.3 us
    reduce_scatter x1, waiting for transfers between devices, shards(): lax.psum_scatter(grad_in, ('seq', 'batch'), scatter_dimension=0, tiled=True)  65.6 us
    mul x32, other arithmetic, combine_affine(): return (earlier[0] * later[0], later[0] * earlier[1] + later[1])  55.8 us
  transfers between devices with their start and end apart: 10, of which 4 were waited for; matrix products, arithmetic and copies ran while one was open for 59% of the time, Pallas kernels for 0%

commit v1 on v0

--- a/solution.py
+++ b/solution.py
@@ -1,20 +1,762 @@
+import functools
+
 import jax
 import jax.numpy as jnp
 from jax import lax
+from jax.experimental import pallas as pl
+from jax.experimental.pallas import tpu as pltpu
 from jax.sharding import PartitionSpec as P
 
 D = 512
 H = 1024
 F = 2048
 STEP = 5
-
-
 EPS = 1e-06
 ADAM_EPS = 1e-08
 BETA_ONE = 0.5
 BETA_TWO = 0.5
 DECAY = 0.1
 VEC_RATE = 1.5
+MESH = pl.DeviceIdType.MESH
+F32 = jnp.float32
+BF16 = jnp.bfloat16
+SUB = 8
+LANES = 128
+SEQS = 3
+
+NN = (((1,), (0,)), ((), ()))
+NT = (((1,), (1,)), ((), ()))
+TN = (((0,), (0,)), ((), ()))
+
+
+def dot(a, b, dims=NN):
+    return lax.dot_general(a, b, dims, preferred_element_type=F32)
+
+
+def tiles(v):
+    return v.reshape(v.shape[0] // SUB, SUB, v.shape[1])
+
+
+def flat(v):
+    return v.reshape(v.shape[0] * SUB, v.shape[2])
+
+
+def fold(v):
+    return jnp.sum(tiles(v), axis=0)
+
+
+def row_mean(v):
+    return jnp.mean(v, axis=-1, keepdims=True)
+
+
+IN, OUT, UP, DOWN = range(4)
+
+
+def step_kernel(
+    nz, span,
+    tok_hbm, cot_hbm, start_ref, len_ref, w_in_hbm, w_out_hbm, w_up_hbm, w_down_hbm, vec_ref,
+    block_hbm, ends_ref, grad_hbm, sum_in, sum_out, sum_up, sum_down, sum_vec,
+    cp, mix, win, wout, wup, wdown, upd, cand, st, gl, du, n2, db, mid, gdown, gup,
+    r0o, r0u, r0d, r1ai, r1bi, r1ao, r1bo, r1au, r1bu, r1ad, r1bd,
+    r2ai, r2bi, r2ao, r2bo, r2au, r2bu, r2ad, r2bd,
+    r3ai, r3bi, r3ao, r3bo, r3au, r3bu, r3ad, r3bd,
+    perm, clock, vec8, vgrad, vrecv, halo_out, halo_in, back_out, back_in,
+    sums, sums_in, bsums, bsums_in,
+    io_sem, ag_send, ag_recv, rs_send, rs_recv, v_sem, h_sem, c_send, c_recv, b_send, b_recv, g_sem, free_sem,
+):
+    nj = span // SUB
+    z = lax.axis_index("seq")
+    b = lax.axis_index("batch")
+    y, x, c = b // 4, lax.rem(b // 2, 2), lax.rem(b, 2)
+    me = z * 8 + b
+    ndev = nz * 8
+    px, py, pc = (z, b + 2 - 4 * x), (z, b + 4 - 8 * y), (z, b + 1 - 2 * c)
+    full = (win, wout, wup, wdown)
+    masters = (w_in_hbm, w_out_hbm, w_up_hbm, w_down_hbm)
+    staged = (sum_in, sum_out, sum_up, sum_down)
+
+    def remote(src, dst, ssem, rsem, dev):
+        return pltpu.make_async_remote_copy(
+            src_ref=src, dst_ref=dst, send_sem=ssem, recv_sem=rsem, device_id=dev, device_id_type=MESH
+        )
+
+    loads = [pltpu.make_async_copy(masters[k], staged[k], io_sem.at[k]) for k in range(4)]
+    tok_load = pltpu.make_async_copy(tok_hbm, n2, io_sem.at[4])
+    cot_load = pltpu.make_async_copy(cot_hbm, db, io_sem.at[5])
+    for cpy in loads:
+        cpy.start()
+    tok_load.start()
+    cot_load.start()
+
+    barrier = pltpu.get_barrier_semaphore()
+
+    def greet(i, carry):
+        @pl.when(i != me)
+        def _():
+            pl.semaphore_signal(barrier, inc=1, device_id=(i // 8, lax.rem(i, 8)), device_id_type=MESH)
+        return carry
+
+    lax.fori_loop(0, ndev, greet, 0)
+
+    rows = lax.broadcasted_iota(jnp.int32, (span, span), 0)
+    cols = lax.broadcasted_iota(jnp.int32, (span, span), 1)
+    perm[...] = jnp.where(cols == lax.rem(rows, SUB) * nj + rows // SUB, 1.0, 0.0).astype(BF16)
+    vrow = lax.broadcasted_iota(jnp.int32, (span, LANES), 0)
+    when = lax.rem(vrow, SUB) * nj + vrow // SUB + z * span
+    clock[...] = when.astype(F32)
+
+    def keep_of(s):
+        one = jnp.where(clock[...] < len_ref[s].astype(F32), 1.0, 0.0)
+        return jnp.concatenate([one] * (D // LANES), axis=1)
+
+    own_vec = vec_ref[...].astype(BF16).astype(F32)
+    vec8[:, pl.ds(pl.multiple_of(me * LANES, LANES), LANES)] = jnp.broadcast_to(own_vec, (SUB, LANES))
+    for k in range(4):
+        loads[k].wait()
+        full[k][z, y, x, c] = staged[k][...].astype(BF16)
+
+    pl.semaphore_wait(barrier, ndev - 1)
+
+    mine = vec8.at[:, pl.ds(pl.multiple_of(me * LANES, LANES), LANES)]
+
+    def spread(i, carry):
+        @pl.when(i != me)
+        def _():
+            remote(mine, mine, v_sem.at[0], v_sem.at[1], (i // 8, lax.rem(i, 8))).start()
+        return carry
+
+    lax.fori_loop(0, ndev, spread, 0)
+
+    def half(k, h):
+        n = full[k].shape[-1] // 2
+        return slice(h * n, (h + 1) * n)
+
+    def ag_z(k):
+        block = full[k].at[z, y, x, c]
+        return [
+            remote(block, block, ag_send.at[k, dz - 1], ag_recv.at[k, dz - 1], (lax.rem(z + dz, nz), b))
+            for dz in range(1, nz)
+        ]
+
+    def ag_1(k):
+        one = full[k].at[:, y, x, c, :, half(k, 0)]
+        two = full[k].at[:, y, x, c, :, half(k, 1)]
+        return [
+            remote(one, one, ag_send.at[k, 3], ag_recv.at[k, 3], px),
+            remote(two, two, ag_send.at[k, 4], ag_recv.at[k, 4], py),
+        ]
+
+    def ag_2(k):
+        one = full[k].at[:, y, :, c, :, half(k, 0)]
+        two = full[k].at[:, :, x, c, :, half(k, 1)]
+        return [
+            remote(one, one, ag_send.at[k, 5], ag_recv.at[k, 5], py),
+            remote(two, two, ag_send.at[k, 6], ag_recv.at[k, 6], px),
+        ]
+
+    def ag_c(k):
+        block = full[k].at[:, :, :, c]
+        return [remote(block, block, ag_send.at[k, 7], ag_recv.at[k, 7], pc)]
+
+    stages = (ag_z, ag_1, ag_2, ag_c)
+
+    def ag_start(k, stage):
+        for cpy in stages[stage](k):
+            cpy.start()
+
+    def ag_wait(k, stage):
+        for cpy in stages[stage](k):
+            cpy.wait_recv()
+
+    def ag_next(k, stage):
+        ag_wait(k, stage - 1)
+        ag_start(k, stage)
+
+    def ag_left(k):
+        for stage in stages:
+            for cpy in stage(k):
+                cpy.wait_send()
+
+    for k in (IN, OUT, UP, DOWN):
+        ag_start(k, 0)
+
+    tok_load.wait()
+    for s in range(SEQS):
+        gdown[s] = dot(perm[...], n2[s]).astype(BF16).reshape(gdown.shape[1:])
+    cot_load.wait()
+    for s in range(SEQS):
+        cp[s] = dot(perm[...], db[s]).astype(BF16)
+    for s in range(SEQS):
+        keep = keep_of(s)
+        db[s] = (cp[s].astype(F32) * keep).astype(BF16)
+
+    rest = vec8.at[:, 0:(ndev - 1) * LANES]
+    remote(rest, rest, v_sem.at[0], v_sem.at[1], pc).wait_recv()
+    ag_next(IN, 1)
+    g_one = vec8[:, 0:D]
+    g_two = vec8[:, D:2 * D]
+    taps = [vec8[:, (2 + k) * D:(3 + k) * D] for k in range(4)]
+
+    def unit_of(v):
+        scale = lax.rsqrt(row_mean(v * v) + EPS)
+        return v * scale, scale
+
+    sub0 = lax.broadcasted_iota(jnp.int32, (SUB, D), 0)
+    for s in range(SEQS):
+        unit, _ = unit_of(gdown[s].reshape(span, D).astype(F32))
+        normed = (tiles(unit) * g_one).astype(BF16).astype(F32)
+        upd[s, 3 * SUB:3 * SUB + span] = flat(normed)
+        for i in range(3):
+            r = 3 * s + i
+            halo_out[r:r + 1, :] = upd[s, span + i * SUB + SUB - 1:span + i * SUB + SUB, :]
+    send_halo = remote(halo_out, halo_in, h_sem.at[0], h_sem.at[1], (lax.rem(z + 1, nz), b))
+    send_halo.start()
+    ag_next(OUT, 1)
+    ag_next(IN, 2)
+    send_halo.wait_recv()
+    for s in range(SEQS):
+        for i in range(3):
+            r = 3 * s + i
+            tile = pltpu.roll(upd[s, span + i * SUB:span + (i + 1) * SUB, :], 1, 0)
+            edge = jnp.where(z > 0, halo_in[r:r + 1, :], 0.0)
+            upd[s, i * SUB:(i + 1) * SUB] = jnp.where(sub0 == 0, edge, tile)
+    for s in range(SEQS):
+        total = taps[0] * tiles(upd[s, 0:span])
+        for k in range(1, 4):
+            total = total + taps[k] * tiles(upd[s, k * SUB:k * SUB + span])
+        mix[s] = flat(total).astype(BF16)
+    ag_next(UP, 1)
+    ag_next(OUT, 2)
+    ag_next(IN, 3)
+    ag_next(DOWN, 1)
+    ag_next(UP, 2)
+    ag_next(OUT, 3)
+    ag_wait(IN, 3)
+
+    def weight(k, *at):
+        v = full[k][at] if at else full[k][...]
+        return v
+
+    def cols_of(k, lo, hi):
+        v = full[k][:, :, :, :, :, lo:hi]
+        return v.reshape(v.shape[0] * 8 * v.shape[4], hi - lo)
+
+    def all_of(k):
+        v = full[k][...]
+        return v.reshape(v.shape[0] * 8 * v.shape[4], v.shape[5])
+
+    def two(ref, s, j):
+        at = pl.multiple_of(j * SUB, SUB)
+        return ref[s, pl.ds(at, SUB), :], ref[s, pl.ds(at + span, SUB), :]
+
+    lane_sub = lax.broadcasted_iota(jnp.int32, (SUB, D), 0)
+
+    def project(s, carry):
+        keep = keep_of(s)
+        rows_in = mix[s]
+        for hh in range(2):
+            bias = vec8[:, 6 * D + hh * D:6 * D + (hh + 1) * D]
+            gate = tiles(dot(rows_in, cols_of(IN, hh * D, (hh + 1) * D))) + bias
+            upd[s, hh * span:(hh + 1) * span] = flat(jax.nn.sigmoid(gate)) * keep
+            cand[s, hh * span:(hh + 1) * span] = dot(rows_in, cols_of(IN, H + hh * D, H + (hh + 1) * D))
+        return carry
+
+    lax.fori_loop(0, SEQS, project, 0)
+
+    def inclusive(keep, drive, reverse):
+        for d in (1, 2, 4):
+            by = SUB - d if reverse else d
+            inside = lane_sub < SUB - d if reverse else lane_sub >= d
+            k2 = jnp.where(inside, pltpu.roll(keep, by, 0), 1.0)
+            d2 = jnp.where(inside, pltpu.roll(drive, by, 0), 0.0)
+            drive = drive + keep * d2
+            keep = keep * k2
+        return keep, drive
+
+    def exclusive(keep, drive, reverse):
+        by = SUB - 1 if reverse else 1
+        edge = lane_sub == (SUB - 1 if reverse else 0)
+        return (
+            jnp.where(edge, 1.0, pltpu.roll(keep, by, 0)),
+            jnp.where(edge, 0.0, pltpu.roll(drive, by, 0)),
+        )
+
+    def scan_totals(s):
+        def body(j, carry):
+            u = two(upd, s, j)
+            v = two(cand, s, j)
+            out = []
+            for hh in range(2):
+                a, d = carry[2 * hh], carry[2 * hh + 1]
+                out += [a * (1.0 - u[hh]), d + u[hh] * (v[hh] - d)]
+            return tuple(out)
+
+        one, zero = jnp.ones((SUB, D), F32), jnp.zeros((SUB, D), F32)
+        return lax.fori_loop(0, nj, body, (one, zero, one, zero), unroll=4)
+
+    prefix = []
+    for s in range(SEQS):
+        a0, d0, a1, d1 = scan_totals(s)
+        for hh, (a, d) in enumerate(((a0, d0), (a1, d1))):
+            a, d = inclusive(a, d, False)
+            sums[s:s + 1, hh * D:(hh + 1) * D] = a[SUB - 1:SUB, :]
+            sums[SEQS + s:SEQS + s + 1, hh * D:(hh + 1) * D] = d[SUB - 1:SUB, :]
+            prefix.append(exclusive(a, d, False))
+
+    def carry_copy(src, dst, ssem, rsem, dz):
+        return remote(src, dst.at[z], ssem.at[dz], rsem.at[z], (z + dz, b))
+
+    for dz in range(1, nz):
+        @pl.when(z + dz < nz)
+        def _():
+            carry_copy(sums, sums_in, c_send, c_recv, dz).start()
+
+    ag_next(DOWN, 2)
+    ag_next(UP, 3)
+
+    def enter_from(i, carry):
+        remote(sums, sums_in.at[i], c_send.at[0], c_recv.at[i], pc).wait_recv()
+        got = sums_in[i]
+        return got[0:SEQS] * carry + got[SEQS:2 * SEQS]
+
+    entering = lax.fori_loop(0, z, enter_from, start_ref[...])
+
+    for s in range(SEQS):
+        def body(i, carry):
+            hs = list(carry)
+            lows = [[], []]
+            for jj in range(2):
+                j = i * 2 + jj
+                at = pl.multiple_of(j * SUB, SUB)
+                u = two(upd, s, j)
+                v = two(cand, s, j)
+                for hh in range(2):
+                    moved = u[hh] * (v[hh] - hs[hh])
+                    hs[hh] = hs[hh] + moved
+                    cand[s, pl.ds(at + hh * span, SUB), :] = moved * (1.0 - u[hh])
+                    lows[hh].append(hs[hh])
+            at = pl.multiple_of(i * 2 * SUB, 2 * SUB)
+            for hh in range(2):
+                st[s, pl.ds(at, 2 * SUB), hh * D:(hh + 1) * D] = jnp.concatenate(lows[hh], axis=0).astype(BF16)
+            return tuple(hs)
+
+        init = []
+        for hh in range(2):
+            ek, ed = prefix[2 * s + hh]
+            init.append(ek * entering[s:s + 1, hh * D:(hh + 1) * D] + ed)
+        ended = lax.fori_loop(0, nj // 2, body, tuple(init), unroll=2)
+        for hh in range(2):
+            ends_ref[s, :, hh * D:(hh + 1) * D] = ended[hh][SUB - 1:SUB, :]
+
+    ag_next(DOWN, 3)
+    ag_wait(OUT, 3)
+    ag_wait(UP, 3)
+    ag_wait(DOWN, 3)
+
+    root = 0.7978845608028654
+    cubic = 0.044715
+
+    def ffn_one(s, carry):
+        keep = keep_of(s)
+        middle = gdown[s].reshape(span, D).astype(F32) + keep * dot(st[s], all_of(OUT))
+        mid[s] = middle
+        scale = lax.rsqrt(row_mean(middle * middle) + EPS)
+        low = flat(tiles(middle * scale) * g_two).astype(BF16)
+        n2[s] = low
+        d_branch = db[s]
+        for q in range(F // D):
+            pre = dot(low, cols_of(UP, q * D, (q + 1) * D))
+            d_gelu = dot(d_branch, wdown[q].reshape(F // nz, D), NT)
+            sq = pre * pre
+            t = jnp.tanh(root * (pre + cubic * (pre * sq)))
+            hp = 0.5 * (1.0 + t)
+            gl[s, :, q * D:(q + 1) * D] = (pre * hp).astype(BF16)
+            slope = hp + (0.5 * root) * pre * (1.0 - t * t) * (1.0 + (3.0 * cubic) * sq)
+            du[s, :, q * D:(q + 1) * D] = (slope * d_gelu).astype(BF16)
+        return carry
+
+    lax.fori_loop(0, SEQS, ffn_one, 0)
+
+    partial = (wup, wout, gup, gdown)
+    r0 = (r0u, r0o, r0u, r0d)
+    r1 = ((r1ai, r1bi), (r1ao, r1bo), (r1au, r1bu), (r1ad, r1bd))
+    r2 = ((r2ai, r2bi), (r2ao, r2bo), (r2au, r2bu), (r2ad, r2bd))
+    r3 = ((r3ai, r3bi), (r3ao, r3bo), (r3au, r3bu), (r3ad, r3bd))
+    finals = (sum_in, sum_out, sum_up, sum_down)
+
+    def rs_copies(k, stage):
+        g, ss, rr = partial[k], rs_send, rs_recv
+        if stage == 0:
+            return [remote(g.at[:, :, :, 1 - c], r0[k], ss.at[k, 0], rr.at[k, 0], pc)]
+        if stage == 1:
+            return [
+                remote(r0[k].at[:, 1 - y, :, :, half(k, 0)], r1[k][0], ss.at[k, 1], rr.at[k, 1], py),
+                remote(r0[k].at[:, :, 1 - x, :, half(k, 1)], r1[k][1], ss.at[k, 2], rr.at[k, 2], px),
+            ]
+        if stage == 2:
+            return [
+                remote(r1[k][0].at[:, 1 - x], r2[k][0], ss.at[k, 3], rr.at[k, 3], px),
+                remote(r1[k][1].at[:, 1 - y], r2[k][1], ss.at[k, 4], rr.at[k, 4], py),
+            ]
+        out = []
+        for dz in range(1, nz):
+            to = lax.rem(z + dz, nz)
+            for h in range(2):
+                at = 5 + 2 * (dz - 1) + h
+                out.append(remote(r2[k][h].at[to], r3[k][h].at[dz - 1], ss.at[k, at], rr.at[k, at], (to, b)))
+        return out
+
+    def rs_start(k, stage):
+        for cpy in rs_copies(k, stage):
+            cpy.start()
+
+    def rs_next(k, stage):
+        for cpy in rs_copies(k, stage - 1):
+            cpy.wait_recv()
+        if stage == 1:
+            r0[k][...] = (r0[k][...].astype(F32) + partial[k][:, :, :, c].astype(F32)).astype(BF16)
+        elif stage == 2:
+            r1[k][0][...] = (r1[k][0][...].astype(F32) + r0[k][:, y, :, :, half(k, 0)].astype(F32)).astype(BF16)
+            r1[k][1][...] = (r1[k][1][...].astype(F32) + r0[k][:, :, x, :, half(k, 1)].astype(F32)).astype(BF16)
+        elif stage == 3:
+            r2[k][0][...] = (r2[k][0][...].astype(F32) + r1[k][0][:, x].astype(F32)).astype(BF16)
+            r2[k][1][...] = (r2[k][1][...].astype(F32) + r1[k][1][:, y].astype(F32)).astype(BF16)
+        else:
+            for h in range(2):
+                total = r2[k][h][z].astype(F32)
+                for i in range(nz - 1):
+                    total = total + r3[k][h][i].astype(F32)
+                finals[k][:, half(k, h)] = total
+        if stage < 4:
+            rs_start(k, stage)
+
+    def whole(ref, lo, hi):
+        v = ref[:, :, lo:hi]
+        return v.reshape(SEQS * span, hi - lo)
+
+    def grad_down(q, carry):
+        qs = pl.multiple_of(q * D, D)
+        v = gl[:, :, pl.ds(qs, D)].reshape(SEQS * span, D)
+        g = dot(v, db[...].reshape(SEQS * span, D), TN)
+        gdown[pl.ds(q, 1)] = g.astype(BF16).reshape((1,) + gdown.shape[1:])
+        return carry
+
+    lax.fori_loop(0, nz, grad_down, 0)
+    rs_start(DOWN, 0)
+    low_all = n2[...].reshape(SEQS * span, D)
+    for q in range(F // D):
+        g = dot(low_all, whole(du, q * D, (q + 1) * D), TN)
+        gup[:, :, :, :, :, q * D:(q + 1) * D] = g.astype(BF16).reshape(gup.shape[:5] + (D,))
+    rs_start(UP, 0)
+    tok_load.start()
+    rs_next(DOWN, 1)
+
+    def ffn_two(s, carry):
+        keep = keep_of(s)
+        middle = mid[s]
+        gy = cp[s].astype(F32)
+        scale = lax.rsqrt(row_mean(middle * middle) + EPS)
+        unit = middle * scale
+        block = (middle + keep * dot(gl[s], all_of(DOWN))).astype(BF16)
+        d_low = dot(du[s], all_of(UP), NT)
+        vgrad[:, D:2 * D] += fold(d_low * unit)
+        e = flat(tiles(d_low) * g_two)
+        d_middle = gy + scale * (e - unit * row_mean(e * unit))
+        mid[s] = d_middle
+        d_mixer = (d_middle * keep).astype(BF16)
+        db[s] = d_mixer
+        cp[s] = dot(perm[...], block, TN).astype(BF16)
+        gl[s, :, 0:H] = dot(d_mixer, all_of(OUT), NT).astype(BF16)
+        return carry
+
+    vgrad[...] = jnp.zeros_like(vgrad)
+    lax.fori_loop(0, SEQS, ffn_two, 0)
+    block_store = pltpu.make_async_copy(cp, block_hbm, io_sem.at[6])
+    block_store.start()
+
+    def two_low(s, i):
+        at = pl.multiple_of(i * 2 * SUB, 2 * SUB)
+        v = gl[s, pl.ds(at, 2 * SUB), 0:H].astype(F32)
+        return [[v[jj * SUB:(jj + 1) * SUB, hh * D:(hh + 1) * D] for hh in range(2)] for jj in range(2)]
+
+    bprefix = []
+    for s in range(SEQS):
+        def body(k, carry):
+            i = nj // 2 - 1 - k
+            vals = list(carry)
+            ds = two_low(s, i)
+            for jj in (1, 0):
+                u = two(upd, s, i * 2 + jj)
+                for hh in range(2):
+                    om = 1.0 - u[hh]
+                    vals[2 * hh] = vals[2 * hh] * om
+                    vals[2 * hh + 1] = om * (ds[jj][hh] + vals[2 * hh + 1])
+            return tuple(vals)
+
+        one, zero = jnp.ones((SUB, D), F32), jnp.zeros((SUB, D), F32)
+        a0, d0, a1, d1 = lax.fori_loop(0, nj // 2, body, (one, zero, one, zero), unroll=2)
+        for hh, (a, d) in enumerate(((a0, d0), (a1, d1))):
+            a, d = inclusive(a, d, True)
+            bsums[s:s + 1, hh * D:(hh + 1) * D] = a[0:1, :]
+            bsums[SEQS + s:SEQS + s + 1, hh * D:(hh + 1) * D] = d[0:1, :]
+            bprefix.append(exclusive(a, d, True))
+    for dz in range(1, nz):
+        @pl.when(z - dz >= 0)
+        def _():
+            remote(bsums, bsums_in.at[z], b_send.at[dz], b_recv.at[z], (z - dz, b)).start()
+
+    ag_left(OUT)
+    def grad_out(q, carry):
+        qs = pl.multiple_of(q * (H // nz), H // nz)
+        v = st[:, :, pl.ds(qs, H // nz)].reshape(SEQS * span, H // nz)
+        g = dot(v, db[...].reshape(SEQS * span, D), TN)
+        wout[pl.ds(q, 1)] = g.astype(BF16).reshape((1,) + wout.shape[1:])
+        return carry
+
+    lax.fori_loop(0, nz, grad_out, 0)
+    rs_start(OUT, 0)
+    rs_next(UP, 1)
+    rs_next(DOWN, 2)
+
+    def leave_from(k, carry):
+        i = nz - 1 - k
+        remote(bsums, bsums_in.at[i], b_send.at[0], b_recv.at[i], pc).wait_recv()
+        got = bsums_in[i]
+        return got[0:SEQS] * carry + got[SEQS:2 * SEQS]
+
+    leaving = lax.fori_loop(0, nz - 1 - z, leave_from, jnp.zeros((SEQS, H), F32))
+
+    for s in range(SEQS):
+        def body(k, carry):
+            i = nj // 2 - 1 - k
+            vals = list(carry)
+            ds = two_low(s, i)
+            gates, cands = [[None] * 2, [None] * 2], [[None] * 2, [None] * 2]
+            for jj in (1, 0):
+                u = two(upd, s, i * 2 + jj)
+                q = two(cand, s, i * 2 + jj)
+                for hh in range(2):
+                    adj = ds[jj][hh] + vals[hh]
+                    vals[hh] = (1.0 - u[hh]) * adj
+                    gate = adj * q[hh]
+                    vals[2 + hh] = vals[2 + hh] + gate
+                    gates[hh][jj] = gate
+                    cands[hh][jj] = adj * u[hh]
+            at = pl.multiple_of(i * 2 * SUB, 2 * SUB)
+            for hh in range(2):
+                du[s, pl.ds(at, 2 * SUB), hh * D:(hh + 1) * D] = jnp.concatenate(gates[hh], axis=0).astype(BF16)
+                du[s, pl.ds(at, 2 * SUB), H + hh * D:H + (hh + 1) * D] = jnp.concatenate(cands[hh], axis=0).astype(BF16)
+            return tuple(vals)
+
+        init = []
+        for hh in range(2):
+            ek, ed = bprefix[2 * s + hh]
+            init.append(ek * leaving[s:s + 1, hh * D:(hh + 1) * D] + ed)
+        zero = jnp.zeros((SUB, D), F32)
+        done = lax.fori_loop(0, nj // 2, body, tuple(init) + (zero, zero), unroll=2)
+        for hh in range(2):
+            vgrad[:, 6 * D + hh * D:6 * D + (hh + 1) * D] += done[2 + hh]
+
+    ag_left(UP)
+    mix_all = mix[...].reshape(SEQS * span, D)
+    for q in range(2 * H // D):
+        g = dot(mix_all, whole(du, q * D, (q + 1) * D), TN)
+        wup[:, :, :, :, :, q * D:(q + 1) * D] = g.astype(BF16).reshape(wup.shape[:5] + (D,))
+    rs_next(UP, 2)
+    for cpy in rs_copies(UP, 1):
+        cpy.wait_send()
+    pl.semaphore_signal(free_sem, inc=1, device_id=pc, device_id_type=MESH)
+    pl.semaphore_wait(free_sem, 1)
+    rs_start(IN, 0)
+    rs_next(OUT, 1)
+    rs_next(DOWN, 3)
+
+    def back_project(s, carry):
+        upd[s, 0:span] = dot(du[s], all_of(IN), NT)
+        return carry
+
+    lax.fori_loop(0, SEQS, back_project, 0)
+    for s in range(SEQS):
+        for i in range(3):
+            r = 3 * s + i
+            back_out[r:r + 1, :] = upd[s, i * SUB:i * SUB + 1, :]
+    send_back = remote(back_out, back_in, h_sem.at[2], h_sem.at[3], (lax.rem(z + nz - 1, nz), b))
+    send_back.start()
+    rs_next(IN, 1)
+    rs_next(OUT, 2)
+    rs_next(UP, 3)
+    send_back.wait_recv()
+    for s in range(SEQS):
+        for i in range(3):
+            r = 3 * s + i
+            tile = pltpu.roll(upd[s, i * SUB:(i + 1) * SUB, :], SUB - 1, 0)
+            edge = jnp.where(z < nz - 1, back_in[r:r + 1, :], 0.0)
+            upd[s, span + i * SUB:span + (i + 1) * SUB] = jnp.where(sub0 == SUB - 1, edge, tile)
+
+    tok_load.wait()
+
+    def back_norm(s, carry):
+        unit, scale = unit_of(dot(perm[...], n2[s]))
+        normed = (tiles(unit) * g_one).astype(BF16).astype(F32)
+        d_normed = jnp.zeros((nj, SUB, D), F32)
+        for k in range(4):
+            ahead = tiles(upd[s, (3 - k) * SUB:(3 - k) * SUB + span])
+            d_normed = d_normed + taps[k] * ahead
+            vgrad[:, (2 + k) * D:(3 + k) * D] += jnp.sum(normed * ahead, axis=0)
+        vgrad[:, 0:D] += jnp.sum(d_normed * tiles(unit), axis=0)
+        e = flat(d_normed * g_one)
+        out = mid[s] + scale * (e - unit * row_mean(e * unit))
+        high = out.astype(BF16)
+        rest_low = (out - high.astype(F32)).astype(BF16)
+        mid[s] = dot(perm[...], high, TN) + dot(perm[...], rest_low, TN)
+        return carry
+
+    lax.fori_loop(0, SEQS, back_norm, 0)
+    grad_store = pltpu.make_async_copy(mid, grad_hbm, io_sem.at[7])
+    grad_store.start()
+
+    def to_owner(i, carry):
+        @pl.when(i != me)
+        def _():
+            src = vgrad.at[:, pl.ds(pl.multiple_of(i * LANES, LANES), LANES)]
+            remote(src, vrecv.at[me], g_sem.at[0], g_sem.at[1], (i // 8, lax.rem(i, 8))).start()
+        return carry
+
+    lax.fori_loop(0, ndev, to_owner, 0)
+    vrecv[me] = vgrad[:, pl.ds(pl.multiple_of(me * LANES, LANES), LANES)]
+    rs_next(IN, 2)
+    rs_next(OUT, 3)
+    rs_next(DOWN, 4)
+    rs_next(UP, 4)
+    rs_next(IN, 3)
+    rs_next(OUT, 4)
+    many = vrecv.at[0:ndev - 1]
+    remote(many, many, g_sem.at[0], g_sem.at[1], pc).wait_recv()
+    sum_vec[...] = jnp.sum(jnp.sum(vrecv[...], axis=0), axis=0, keepdims=True)
+    rs_next(IN, 4)
+
+    for k in range(4):
+        for stage in range(4):
+            if (k, stage) != (UP, 1):
+                for cpy in rs_copies(k, stage):
+                    cpy.wait_send()
+    ag_left(IN)
+    ag_left(DOWN)
+    remote(rest, rest, v_sem.at[0], v_sem.at[1], pc).wait_send()
+    remote(many, many, g_sem.at[0], g_sem.at[1], pc).wait_send()
+    send_halo.wait_send()
+    send_back.wait_send()
+    for dz in range(1, nz):
+        @pl.when(z + dz < nz)
+        def _():
+            carry_copy(sums, sums_in, c_send, c_recv, dz).wait_send()
+
+        @pl.when(z - dz >= 0)
+        def _():
+            remote(bsums, bsums_in.at[z], b_send.at[dz], b_recv.at[z], (z - dz, b)).wait_send()
+    block_store.wait()
+    grad_store.wait()
+
+
+def adam_math(weight, grad, first, second, rate, decay):
+    moment = BETA_ONE * first + (1.0 - BETA_ONE) * grad
+    square = BETA_TWO * second + (1.0 - BETA_TWO) * grad * grad
+    corr_one = 1.0 - BETA_ONE**STEP
+    corr_two = 1.0 - BETA_TWO**STEP
+    direction = moment / corr_one / (jnp.sqrt(square / corr_two) + ADAM_EPS)
+    fresh = weight - rate * (direction + decay * weight)
+    return fresh, moment, square
+
+
+def adam_kernel(rates, *refs):
+    ins, outs = refs[:20], refs[20:]
+    at = 0
+    for k in range(5):
+        rate, decay = rates[k]
+        w, g, m, v = (r[...] for r in ins[4 * k:4 * k + 4])
+        fresh, moment, square = adam_math(w, g, m, v, rate, decay)
+        outs[at][...] = fresh
+        at += 1
+        if k < 4:
+            outs[at][...] = fresh.astype(BF16)
+            at += 1
+        outs[at][...] = moment
+        outs[at + 1][...] = square
+        at += 2
+
+
+def fast_shards(nz, *args):
+    (tokens, cotangent, start, lengths, w_in, w_out, w_up, w_down, vectors,
+     m_in, v_in, m_out, v_out, m_up, v_up, m_down, v_down, m_vec, v_vec) = args
+    span = tokens.shape[1]
+    hbm = pl.BlockSpec(memory_space=pl.ANY)
+    vmem = pl.BlockSpec(memory_space=pltpu.VMEM)
+    smem = pl.BlockSpec(memory_space=pltpu.SMEM)
+    rows = [w.shape[0] for w in (w_in, w_out, w_up, w_down)]
+    cols = [w.shape[1] for w in (w_in, w_out, w_up, w_down)]
+    vec_row = vectors.reshape(1, LANES)
+
+    def S(*shape, dtype=F32):
+        return jax.ShapeDtypeStruct(shape, dtype)
+
+    def low(*shape):
+        return pltpu.VMEM(shape, BF16)
+
+    def wide(*shape):
+        return pltpu.VMEM(shape, F32)
+
+    dma = pltpu.SemaphoreType.DMA
+    nsend = 5 + 2 * (nz - 1)
+    ndev = nz * 8
+    scratch = [
+        low(SEQS, span, D), low(SEQS, span, D),
+        *[low(nz, 2, 2, 2, r, n) for r, n in zip(rows, cols)],
+        wide(SEQS, 2 * span, D), wide(SEQS, 2 * span, D),
+        low(SEQS, span, H), low(SEQS, span, F), low(SEQS, span, F),
+        low(SEQS, span, D), low(SEQS, span, D), wide(SEQS, span, D),
+        low(nz, 2, 2, 2, rows[3], cols[3]), low(nz, 2, 2, 2, rows[2], cols[2]),
+        *[low(nz, 2, 2, r, n) for r, n in zip(rows[1:], cols[1:])],
+        *[low(nz, 2, r, n // 2) for r, n in zip(rows, cols) for _ in range(2)],
+        *[low(nz, r, n // 2) for r, n in zip(rows, cols) for _ in range(2)],
+        *[low(nz - 1, r, n // 2) for r, n in zip(rows, cols) for _ in range(2)],
+        low(span, span), wide(span, LANES),
+        wide(SUB, 8 * D), wide(SUB, 8 * D), wide(ndev, SUB, LANES),
+        wide(16, D), wide(16, D), wide(16, D), wide(16, D),
+        wide(SUB, H), wide(nz, SUB, H), wide(SUB, H), wide(nz, SUB, H),
+        dma((8,)), dma((4, 8)), dma((4, 8)), dma((4, nsend)), dma((4, nsend)),
+        dma((2,)), dma((4,)), dma((nz,)), dma((nz,)), dma((nz,)), dma((nz,)), dma((2,)), pltpu.SemaphoreType.REGULAR,
+    ]
+    block, ends, grad, s_in, s_out, s_up, s_down, s_vec = pl.pallas_call(
+        functools.partial(step_kernel, nz, span),
+        out_shape=[
+            S(SEQS, span, D, dtype=BF16), S(SEQS, 1, H), S(SEQS, span, D),
+            *[S(r, n) for r, n in zip(rows, cols)], S(1, LANES),
+        ],
+        in_specs=[hbm, hbm, vmem, smem, hbm, hbm, hbm, hbm, vmem],
+        out_specs=[hbm, vmem, hbm, vmem, vmem, vmem, vmem, vmem],
+        scratch_shapes=scratch,
+        compiler_params=pltpu.CompilerParams(
+            collective_id=0, has_side_effects=True, vmem_limit_bytes=64 * 2**20 - 2**18
+        ),
+    )(tokens, cotangent, start, lengths, w_in, w_out, w_up, w_down, vec_row)
+
+    rates = ((D**-0.5, DECAY), (H**-0.5, DECAY), (D**-0.5, DECAY), (F**-0.5, DECAY), (VEC_RATE, 0.0))
+    outs = []
+    for k in range(4):
+        outs += [S(rows[k], cols[k]), S(rows[k], cols[k], dtype=BF16), S(rows[k], cols[k]), S(rows[k], cols[k])]
+    outs += [S(1, LANES)] * 3
+    fresh = pl.pallas_call(
+        functools.partial(adam_kernel, rates),
+        out_shape=outs,
+        in_specs=[vmem] * 20,
+        out_specs=[vmem] * 19,
+        compiler_params=pltpu.CompilerParams(vmem_limit_bytes=32 * 2**20),
+    )(
+        w_in, s_in, m_in, v_in, w_out, s_out, m_out, v_out, w_up, s_up, m_up, v_up,
+        w_down, s_down, m_down, v_down,
+        vec_row, s_vec, m_vec.reshape(1, LANES), v_vec.reshape(1, LANES),
+    )
+    return (block, ends, grad, *fresh[:16], *[v.reshape(LANES) for v in fresh[16:]])
 
 
 def entering_2(value, axis, combine, identity, reverse):
@@ -276,8 +1018,10 @@
         P(("seq", "batch")),
         P(("seq", "batch")),
     )
+    nz, nb = mesh.shape["seq"], mesh.shape["batch"]
+    fits = nb == 8 and nz == 4
     return jax.shard_map(
-        shards,
+        functools.partial(fast_shards, nz) if fits else shards,
         mesh=mesh,
         in_specs=placed,
         out_specs=(

time: 1400 us -> 154 us (0.11); the launches traced: 1370 us -> 153 us
  local copies, waits for them, and re-layouts: 736 us -> 19.8 us
  waiting for transfers between devices: 212 us -> 0 us
  other arithmetic: 186 us -> 0 us
  blocking collectives: 136 us -> 0 us
  Pallas kernels: 0 us -> 132 us
  matrix products: 81.3 us -> 0 us
  between operations: 16.8 us -> 0.73 us
    slice x130 -> x0, local copies, waits for them, and re-layouts: 425 us -> none  [the longest x65 276 us: shards(): lax.associative_scan(combine_affine, (shifted, d_states), axis=1, reverse...]
    reduce_scatter x4 -> x0, waiting for transfers between devices: 206 us -> none  [the longest x1 140 us: shards(): lax.psum_scatter(grad_down, ('seq', 'batch'), scatter_dimension=0, tiled=...]
    pad x64 -> x0, local copies, waits for them, and re-layouts: 184 us -> none  [the longest x32 95 us: shards(): lax.associative_scan(combine_affine, (retain, driven), axis=1)]
    pallas_call x0 -> x2, Pallas kernels: none -> 132 us  [the longest x1 131 us: fast_shards(): pl.pallas_call(functools.partial(step_kernel, nz, span), out_shape=[S(SEQ...]
    rev x2 -> x0, local copies, waits for them, and re-layouts: 97 us -> none  [shards(): lax.associative_scan(combine_affine, (shifted, d_states), axis=1, reverse...]
    all_gather x5 -> x0, blocking collectives: 95.3 us -> none  [the longest x4 52.3 us: entering_2(): everything = jax.tree.map(lambda part: lax.all_gather(part, axis), value)]
    dot_general x14 -> x0, matrix products: 81.3 us -> none  [the longest x1 13.6 us: shards(): jnp.einsum('scd,fd->scf', d_branch, full_down, preferred_element_type=f32)]
    add x42 -> x0, other arithmetic: 64.1 us -> none  [the longest x18 32.3 us: shards(): lax.associative_scan(combine_affine, (shifted, d_states), axis=1, reverse...]
  transfers between devices with their start and end apart: 10 -> 0, of which waited for: 4 -> 0; matrix products, arithmetic and copies ran while one was open for 59% -> 0% of each run, Pallas kernels for 0% -> 0%
where the time goes in v1:
time: 154 us; the launch traced here: 153 us
  Pallas kernels  132 us (86%)
  local copies, waits for them, and re-layouts  19.8 us (13%)
    pallas_call x1, Pallas kernels, fast_shards(): pl.pallas_call(functools.partial(step_kernel, nz, span), out_shape=[S(SEQ...  131 us
    unnamed x49, local copies, waits for them, and re-layouts  19.8 us

profile of v1, /device:TPU:0, one launch (start us, length us, event | category | flops | bytes accessed | tf_op | source)
XLA Modules:
  0.0 153.0 jit_solution(7321171807189739180)
XLA Ops:
  0.7 0.0 copy-start
  0.7 0.0 copy-start.3
  0.7 131.1 %shard_map.354 = (bf16[3,512,512]{2,1,0:T(8,128)(2,1)}, f32[3,1,1024]{2,1,0:T(1,128)}, f32[3,512,512]{2,1,0:T(8,128)}, f32[16,2048]{1,0:T(8,128)}, f32[32,512]{1...) custom-call(bf16[3,512,512]{2,1,0:T(8,128)(2,1)} %tok_hbm.1, bf16[3,512,512]{2,1,0:T(8,128)(2,1)} %cot_hbm.1, ...), custom_call_target="tpu_custom_call" | custom-call | tf_op jit(solution)/shard_map/pallas_call | solution.py:729
  131.8 0.0 copy-done
  131.8 0.0 copy-done.3
  131.8 0.0 copy-start.1
  131.8 0.9 copy-done.1
  132.7 0.0 copy-start.2
  132.7 0.9 copy-done.2
  133.6 0.0 copy-start.4
  133.6 0.9 copy-done.4
  134.5 0.0 copy-start.5
  134.5 0.9 copy-done.5
  135.4 0.0 copy-start.6
  135.4 0.9 copy-done.6
  136.3 0.0 copy-start.7
  136.3 0.9 copy-done.7
  137.2 0.0 copy-start.8
  137.2 0.9 copy-done.8
  138.1 0.0 copy-start.9
  138.2 0.9 copy-done.9
  139.1 0.0 copy-start.10
  139.1 0.9 copy-done.10
  140.0 0.0 copy-start.11
  140.0 0.9 copy-done.11
  140.9 0.0 copy-start.12
  140.9 0.9 copy-done.12
  141.8 0.0 copy-start.13
  141.8 0.8 copy-done.13
  142.6 0.0 copy-start.14
  142.6 0.8 copy-done.14
  143.4 0.0 copy-start.15
  143.4 0.8 copy-done.15
  144.3 0.0 copy-start.16
  144.3 0.7 copy-done.16
  144.9 0.0 copy-start.17
  144.9 0.7 copy-done.17
  145.6 0.0 copy-start.18
  145.6 0.7 copy-done.18
  146.3 0.0 copy-start.19
  146.3 0.7 copy-done.19
  146.9 0.0 copy-start.21
  146.9 0.0 copy-start.22
  146.9 1.3 shard_map.355
  148.3 0.6 copy-done.21
  148.9 0.0 copy-start.20
  148.9 1.1 copy.44
  150.0 0.0 copy-done.22
  150.0 0.6 copy.45
  150.6 0.7 copy-done.20
  151.4 1.7 %copy.46 = f32[3,512,512]{2,1,0:T(8,128)} copy(f32[3,512,512]{2,1,0:T(8,128)S(1)} %copy-done.20) | data formatting | bytes 6291456
Async XLA Ops:
  0.7 131.1 %copy-start = (f32[16,2048]{1,0:T(8,128)S(1)}, f32[16,2048]{1,0:T(8,128)}, u32[]{:S(2)}) copy-start(f32[16,2048]{1,0:T(8,128)} %refs_0_.1) | copy-start | bytes 393220
  0.7 131.1 %copy-start.3 = (f32[32,512]{1,0:T(8,128)S(1)}, f32[32,512]{1,0:T(8,128)}, u32[]{:S(2)}) copy-start(f32[32,512]{1,0:T(8,128)} %refs_4_.1) | copy-start | bytes 196612
  131.8 0.9 copy-start.1
  132.7 0.9 copy-start.2
  133.6 0.9 copy-start.4
  134.5 0.9 copy-start.5
  135.4 0.9 copy-start.6
  136.3 0.9 copy-start.7
  137.2 0.9 copy-start.8
  138.1 0.9 copy-start.9
  139.1 0.9 copy-start.10
  140.0 0.9 copy-start.11
  140.9 0.9 copy-start.12
  141.8 0.8 copy-start.13
  142.6 0.8 copy-start.14
  143.4 0.8 copy-start.15
  144.3 0.7 copy-start.16
  144.9 0.7 copy-start.17
  145.6 0.7 copy-start.18
  146.3 0.7 copy-start.19
  146.9 2.0 %copy-start.21 = (bf16[3,512,512]{2,1,0:T(8,128)(2,1)S(1)}, bf16[3,512,512]{2,1,0:T(8,128)(2,1)}, u32[]{:S(2)}) copy-start(bf16[3,512,512]{2,1,0:T(8,128)(2,1)} %get-tuple-element.98) | copy-start | bytes 4718596
  146.9 3.1 %copy-start.22 = (f32[3,1,1024]{2,1,0:T(1,128)S(1)}, f32[3,1,1024]{2,1,0:T(1,128)}, u32[]{:S(2)}) copy-start(f32[3,1,1024]{2,1,0:T(1,128)} %get-tuple-element.99) | copy-start | bytes 36868
  148.9 2.5 %copy-start.20 = (f32[3,512,512]{2,1,0:T(8,128)S(1)}, f32[3,512,512]{2,1,0:T(8,128)}, u32[]{:S(2)}) copy-start(f32[3,512,512]{2,1,0:T(8,128)} %get-tuple-element.100) | copy-start | bytes 9437188
